TPU v7x, 128 devices: a whole 4x4x4 slice. The times are simulated.
128 devices in a mesh: row: 32 (over y, z, core), col: 4 (over x).
Axes of the slice: x: 4, y: 4, z: 4, core: 2. Of those that a mesh axis runs over, the one named last changes fastest.
Arguments:
- tile_values: bfloat16 [5632, 4, 256, 256], P('row', 'col'), may hold values from -0.375 to 0.375
- tile_rows: int32 [5632, 4], P('row', 'col'), may hold values from 0 to 15, as said below
- tile_source: int32 [5632, 4], P('row', 'col'), may hold values from 0 to 31
- tile_slot: int32 [5632, 4], P('row', 'col'), may hold values from 0 to 1
- send_lists: int32 [32, 4, 32, 2], P('row', 'col'), may hold values from 0 to 7
- basis_blocks: bfloat16 [256, 4, 256, 256], P('row', 'col'), may hold values from -6 to 6
Outputs:
- new_basis: float32 [131072, 256], P(('row', 'col'))
- triangle: float32 [256, 256], replicated
Inputs may be any that keep to these rules, and one draw needn't show every extreme that they name: `tile_rows`: in every slab and group each of the 16 block rows holds at least one tile.
All inputs are finite; a program needn't handle non-finite values.
Results may differ from a plain program's by a relative error of at most 0.0015.
Values may be sent and summed in bfloat16 or wider, within the bound.
No kernel may reach another device: no remote copies, remote signals or barrier semaphores. Data moves between devices by JAX's collectives and lax.ppermute only.
A program may use at most 256 MiB of HBM per device.

v0:
```python
import jax
import jax.numpy as jnp
from jax import lax
from jax.sharding import PartitionSpec as P

BR_DEV = 16


def upper_factor(gram):
    width = gram.shape[0]
    index = jnp.arange(width, dtype=jnp.int32)

    def row_fill(j, upper):
        unit = (index == j).astype(jnp.float32)
        known = jnp.dot(upper, unit, precision=lax.Precision.HIGHEST)
        target = lax.dynamic_index_in_dim(gram, j, 0, keepdims=False)
        residue = target - jnp.dot(known, upper, precision=lax.Precision.HIGHEST)
        pivot = jnp.sqrt(lax.dynamic_index_in_dim(residue, j, 0, keepdims=False))
        filled = jnp.where(index >= j, residue / pivot, jnp.float32(0.0))
        return upper + unit[:, None] * filled[None, :]

    return lax.fori_loop(0, width, row_fill, jnp.zeros((width, width), jnp.float32))


def upper_inverse(upper):
    width = upper.shape[0]
    index = jnp.arange(width, dtype=jnp.int32)

    def row_step(step, inverse):
        i = (width - 1 - step).astype(jnp.int32)
        row_now = lax.dynamic_index_in_dim(upper, i, 0, keepdims=False)
        pivot = lax.dynamic_index_in_dim(row_now, i, 0, keepdims=False)
        unit = (index == i).astype(jnp.float32)
        solved = (unit - jnp.dot(row_now, inverse, precision=lax.Precision.HIGHEST)) / pivot
        return jnp.where((index == i)[:, None], solved[None, :], inverse)

    return lax.fori_loop(0, width, row_step, jnp.zeros((width, width), jnp.float32))


def local(tile_values, tile_rows, tile_source, tile_slot, send_lists, basis_blocks):
    values = tile_values[:, 0]
    blocks_row = tile_rows[:, 0]
    source = tile_source[:, 0]
    slotted = tile_slot[:, 0]
    owned = basis_blocks[:, 0]
    slot_count = send_lists.shape[3]
    rank_width = owned.shape[2]
    outgoing = owned[send_lists[0, 0]]
    arrived = lax.all_to_all(outgoing, "row", split_axis=0, concat_axis=0, tiled=True)
    flatten = arrived.reshape(-1, arrived.shape[2], arrived.shape[3])
    chosen = flatten[source * slot_count + slotted]
    product = jnp.einsum("tij,tjk->tik", values, chosen, preferred_element_type=jnp.float32)
    selector = (blocks_row[None, :] == jnp.arange(BR_DEV, dtype=jnp.int32)[:, None]).astype(
        jnp.float32
    )
    partial_value = jnp.einsum("bt,tik->bik", selector, product, precision=lax.Precision.HIGHEST)
    partial_value = partial_value.reshape(-1, rank_width)
    local_y = lax.psum_scatter(partial_value, "col", scatter_dimension=0, tiled=True)
    gram = jnp.dot(local_y.T, local_y, precision=lax.Precision.HIGHEST)
    summed = lax.psum(gram, ("row", "col"))
    upper = upper_factor(summed)
    cells_all = local_y.shape[0] * lax.axis_size("row") * lax.axis_size("col")
    scale = jnp.sqrt(jnp.float32(cells_all))
    solved = jnp.dot(local_y, upper_inverse(upper), precision=lax.Precision.HIGHEST)
    return (solved * scale, upper / scale)


def solution(mesh):
    return jax.shard_map(
        local,
        mesh=mesh,
        in_specs=(
            P("row", "col", None, None),
            P("row", "col"),
            P("row", "col"),
            P("row", "col"),
            P("row", "col", None, None),
            P("row", "col", None, None),
        ),
        out_specs=(P(("row", "col"), None), P()),
        check_vma=False,
    )
```

profile of v0, /device:TPU:1, one launch (start us, length us, event | category | flops | bytes accessed | tf_op | source)
XLA Modules:
  0.0 1576.3 jit_solution(10319401639767442812)
XLA Ops:
  7.2 0.8 compare_select_fusion.2
  8.4 5.5 gather_fusion
  13.9 9.6 all-to-all-start
  23.7 108.4 %all-to-all-done = bf16[32,2,256,256]{3,2,1,0:T(8,128)(2,1)} async-done(((bf16[32,2,256,256]{3,2,1,0:T(8,128)(2,1)}), bf16[32,2,256,256]{3,2,1,0:T(8,128)(2,1)}, u32[]{:S(2)}, u32[]{:S(2)}) %all-to-all-start) | async-done | bytes 8388640 | tf_op jit(solution)/shard_map/all_to_all | solution.py:49
  132.1 13.8 gather_fusion.1
  145.9 37.6 %fusion.24 = f32[176,256,256]{2,1,0:T(8,128)} fusion(bf16[176,256,256]{2,1,0:T(8,128)(2,1)} %gather_fusion.1, bf16[176,1,256,256]{3,2,1,0:T(8,128)(2,1)} %param.10), kind=kOutput, calls=%fused_computation.32 | convolution fusion | flops 5905580032 | bytes 92274688 | tf_op jit(solution)/shard_map/tij,tjk->tik/dot_general | solution.py:52
  183.5 46.6 %copy.11 = f32[176,256,256]{1,0,2:T(8,128)} copy(f32[176,256,256]{2,1,0:T(8,128)} %fusion.24) | data formatting | bytes 92274688 | tf_op jit(solution)/shard_map/tij,tjk->tik/dot_general | solution.py:52
  230.1 20.4 %fusion.22 = f32[16,256,256]{2,0,1:T(8,128)S(1)} fusion(f32[176,256,256]{1,0,2:T(8,128)} %copy.11, s32[176]{0:T(256)S(1)} %bitcast.63), kind=kOutput, calls=%fused_computation.30 | convolution fusion | flops 2214595328 | bytes 50332352 | tf_op jit(solution)/shard_map/bt,tik->bik/dot_general | solution.py:56
  250.5 4.4 copy.10
  255.1 61.9 %reduce-scatter.2.cloned.1.call-done = f32[1024,256]{1,0:T(8,128)} async-done(((f32[4096,256]{1,0:T(8,128)}), f32[1024,256]{1,0:T(8,128)}) %reduce-scatter.2.cloned.1.call-update) | async-done | bytes 1048592 | tf_op jit(solution)/shard_map/reduce_scatter | solution.py:58
  317.0 4.1 fusion.29
  321.1 143.2 %all-reduce.2.cloned.1.call-done = f32[256,256]{1,0:T(8,128)} async-done(((f32[256,256]{1,0:T(8,128)}), f32[256,256]{1,0:T(8,128)}) %all-reduce.2.cloned.1.call-update) | async-done | bytes 262160 | tf_op jit(solution)/shard_map/psum | solution.py:60
  464.3 680.8 %while.33 = (s32[]{:T(128)}, f32[256,256]{1,0:T(8,128)S(1)}, f32[256,256]{1,0:T(8,128)}, s32[]{:T(128)}, s32[]{:T(128)}) while((s32[]{:T(128)}, f32[256,256]{1,0:T(8,128)S(1)}, f32[256,256]{1,0:T(8,128)}, s32[]{:T(128)}, s32[]{:T(128)}) %tuple.80), condition=%wide.region_3.4_spmd.clone.clone, body=%wide.region_2.3_spmd.clone.clone.sunk | while | flops 1902083 | bytes 1063021 | solution.py:22
  467.5 0.7 constant_dynamic-slice_fusion.2
  470.1 0.7 constant_dynamic-slice_fusion.2
  475.4 0.7 constant_dynamic-slice_fusion.2
  478.1 0.7 constant_dynamic-slice_fusion.2
  486.1 0.7 constant_dynamic-slice_fusion.2
  494.1 0.7 constant_dynamic-slice_fusion.2
  496.7 0.7 constant_dynamic-slice_fusion.2
  502.0 0.7 constant_dynamic-slice_fusion.2
  504.7 0.7 constant_dynamic-slice_fusion.2
  1145.9 420.4 %while.32 = (s32[]{:T(128)}, f32[256,256]{1,0:T(8,128)S(1)}, f32[256,256]{1,0:T(8,128)S(1)}, s32[]{:T(128)}, s32[]{:T(128)}, /*index=5*/s32[]{:T(128)}, s32[]{:T(128)}) while((s32[]{:T(128)}, f32[256,256]{1,0:T(8,128)S(1)}, f32[256,256]{1,0:T(8,128)S(1)}, s32[]{:T(128)}, s32[]{:T(128)}, /*index=5*/s32[]{:T(128)}, s32[]{:T(128)}) %tuple.83), condition=%wide.region_5.6_spmd.clone, body=%wide.region_4.5_spmd.clone.sunk | while | flops 984328 | bytes 792242 | solution.py:37
  1566.2 3.2 convolution_multiply_fusion
  (3597 shorter events, 894.5 us)
Async XLA Ops:
  7.2 1.2 copy-start
  7.2 16.4 %copy-start.4 = (s32[176,1]{0,1:T(1,128)S(1)}, s32[176,1]{0,1:T(1,128)}, u32[]{:S(2)}) copy-start(s32[176,1]{0,1:T(1,128)} %param.12) | copy-start | bytes 2116
  7.2 16.4 %copy-start.3 = (s32[176,1]{0,1:T(1,128)S(1)}, s32[176,1]{0,1:T(1,128)}, u32[]{:S(2)}) copy-start(s32[176,1]{0,1:T(1,128)} %param.13) | copy-start | bytes 2116
  13.9 118.2 %all-to-all-start = ((bf16[32,2,256,256]{3,2,1,0:T(8,128)(2,1)}), bf16[32,2,256,256]{3,2,1,0:T(8,128)(2,1)}, u32[]{:S(2)}, u32[]{:S(2)}) async-start(bf16[32,2,256,256]{3,2,1,0:T(8,128)(2,1)} %bitcast.57), calls=%async_computation | async-start | bytes 16777216 | tf_op jit(solution)/shard_map/all_to_all | solution.py:49
  23.6 293.4 %reduce-scatter.2.cloned.1.call-start = ((), (), s32[]{:S(2)}) async-start(), calls=%async_computation.2 | async-start | bytes 5242880 | tf_op jit(solution)/shard_map/reduce_scatter | solution.py:58
  183.5 46.6 %copy-start.2 = (s32[176,1]{0,1:T(1,128)S(1)}, s32[176,1]{0,1:T(1,128)}, u32[]{:S(2)}) copy-start(s32[176,1]{0,1:T(1,128)} %param.11) | copy-start | bytes 2116
  230.1 1339.3 %copy-start.1 = (bf16[8,1,256,256]{3,2,1,0:T(8,128)(2,1)S(1)}, bf16[8,1,256,256]{3,2,1,0:T(8,128)(2,1)}, u32[]{:S(2)}) copy-start(bf16[8,1,256,256]{3,2,1,0:T(8,128)(2,1)} %param.15) | copy-start | bytes 3145732
  254.9 209.4 %all-reduce.2.cloned.1.call-start = ((), (), s32[]{:S(2)}) async-start(), calls=%async_computation.3 | async-start | bytes 524288 | tf_op jit(solution)/shard_map/psum | solution.py:60
Sparse Core Ops, SparseCore 0:
  255.0 61.9 reduce-scatter.1
  323.0 141.2 all-reduce.1
where the time goes:
time: 1600 us; the launch traced here: 1580 us
  local copies, waits for them, and re-layouts  577 us (36%)
  waiting for transfers between devices  314 us (20%)
  matrix products  233 us (15%)
  other arithmetic  227 us (14%)
  loops' own time  202 us (13%)
    dynamic_slice x256, local copies, waits for them, and re-layouts, row_fill(): target = lax.dynamic_index_in_dim(gram, j, 0, keepdims=False)  190 us
    another operation x1, loops' own time, upper_factor(): lax.fori_loop(0, width, row_fill, jnp.zeros((width, width), jnp.float32))  189 us
    dynamic_slice x256, local copies, waits for them, and re-layouts, row_step(): pivot = lax.dynamic_index_in_dim(row_now, i, 0, keepdims=False)  164 us
    div x256, other arithmetic, row_step(): (unit - jnp.dot(row_now, inverse, precision=lax.Precision.HIGHEST)) / pivot  163 us
    dynamic_slice x256, local copies, waits for them, and re-layouts, row_fill(): pivot = jnp.sqrt(lax.dynamic_index_in_dim(residue, j, 0, keepdims=False))  150 us
    psum x1, waiting for transfers between devices, local(): summed = lax.psum(gram, ('row', 'col'))  143 us
    all_to_all x1, waiting for transfers between devices, local(): lax.all_to_all(outgoing, 'row', split_axis=0, concat_axis=0, tiled=True)  108 us
    reduce_scatter x1, waiting for transfers between devices, local(): lax.psum_scatter(partial_value, 'col', scatter_dimension=0, tiled=True)  61.9 us
  transfers between devices with their start and end apart: 3, of which 3 were waited for; matrix products, arithmetic and copies ran while one was open for 0% of the time, Pallas kernels for 0%

commit v1 on v0

--- a/solution.py
+++ b/solution.py
@@ -57,7 +57,7 @@
     partial_value = partial_value.reshape(-1, rank_width)
     local_y = lax.psum_scatter(partial_value, "col", scatter_dimension=0, tiled=True)
     gram = jnp.dot(local_y.T, local_y, precision=lax.Precision.HIGHEST)
-    summed = lax.psum(gram, ("row", "col"))
+    summed = jnp.sum(lax.all_gather(gram, ("row", "col")), axis=0)
     upper = upper_factor(summed)
     cells_all = local_y.shape[0] * lax.axis_size("row") * lax.axis_size("col")
     scale = jnp.sqrt(jnp.float32(cells_all))

time: 1600 us -> 1390 us (0.87)
  local copies, waits for them, and re-layouts: 577 us -> 408 us
  waiting for transfers between devices: 314 us -> 277 us
    dynamic_slice x256, local copies, waits for them, and re-layouts: 190 us -> 10.5 us  [row_fill(): target = lax.dynamic_index_in_dim(gram, j, 0, keepdims=False)]
    psum x1 -> x0, waiting for transfers between devices: 143 us -> none  [local(): summed = lax.psum(gram, ('row', 'col'))]
    all_gather x0 -> x1, waiting for transfers between devices: none -> 107 us  [local(): summed = jnp.sum(lax.all_gather(gram, ('row', 'col')), axis=0)]
where the time goes in v1:
time: 1390 us; the launch traced here: 1380 us
  local copies, waits for them, and re-layouts  408 us (29%)
  waiting for transfers between devices  277 us (20%)
  other arithmetic  236 us (17%)
  matrix products  232 us (17%)
  loops' own time  205 us (15%)
  between operations  14.2 us (1%)
    another operation x1, loops' own time, upper_factor(): lax.fori_loop(0, width, row_fill, jnp.zeros((width, width), jnp.float32))  193 us
    dynamic_slice x256, local copies, waits for them, and re-layouts, row_step(): pivot = lax.dynamic_index_in_dim(row_now, i, 0, keepdims=False)  174 us
    div x256, other arithmetic, row_step(): (unit - jnp.dot(row_now, inverse, precision=lax.Precision.HIGHEST)) / pivot  160 us
    dynamic_slice x256, local copies, waits for them, and re-layouts, row_fill(): pivot = jnp.sqrt(lax.dynamic_index_in_dim(residue, j, 0, keepdims=False))  151 us
    all_to_all x1, waiting for transfers between devices, local(): lax.all_to_all(outgoing, 'row', split_axis=0, concat_axis=0, tiled=True)  108 us
    all_gather x1, waiting for transfers between devices, local(): summed = jnp.sum(lax.all_gather(gram, ('row', 'col')), axis=0)  107 us
    reduce_scatter x1, waiting for transfers between devices, local(): lax.psum_scatter(partial_value, 'col', scatter_dimension=0, tiled=True)  61.9 us
    dot_general x256, matrix products, row_fill(): residue = target - jnp.dot(known, upper, precision=lax.Precision.HIGHEST)  60.5 us
  transfers between devices with their start and end apart: 3, of which 3 were waited for; matrix products, arithmetic and copies ran while one was open for 0% of the time, Pallas kernels for 0%

profile of v1, /device:TPU:1, one launch (start us, length us, event | category | flops | bytes accessed | tf_op | source)
XLA Modules:
  0.0 1382.2 jit_solution(14344511498001732351)
XLA Ops:
  7.2 0.8 compare_select_fusion.2
  8.4 5.5 gather_fusion
  13.9 9.6 all-to-all-start
  23.7 108.4 %all-to-all-done = bf16[32,2,256,256]{3,2,1,0:T(8,128)(2,1)} async-done(((bf16[32,2,256,256]{3,2,1,0:T(8,128)(2,1)}), bf16[32,2,256,256]{3,2,1,0:T(8,128)(2,1)}, u32[]{:S(2)}, u32[]{:S(2)}) %all-to-all-start) | async-done | bytes 8388640 | tf_op jit(solution)/shard_map/all_to_all | solution.py:49
  132.1 13.8 gather_fusion.1
  145.9 37.6 %fusion.24 = f32[176,256,256]{2,1,0:T(8,128)} fusion(bf16[176,256,256]{2,1,0:T(8,128)(2,1)} %gather_fusion.1, bf16[176,1,256,256]{3,2,1,0:T(8,128)(2,1)} %param.10), kind=kOutput, calls=%fused_computation.32 | convolution fusion | flops 5905580032 | bytes 92274688 | tf_op jit(solution)/shard_map/tij,tjk->tik/dot_general | solution.py:52
  183.5 46.5 %copy.11 = f32[176,256,256]{1,0,2:T(8,128)} copy(f32[176,256,256]{2,1,0:T(8,128)} %fusion.24) | data formatting | bytes 92274688 | tf_op jit(solution)/shard_map/tij,tjk->tik/dot_general | solution.py:52
  230.0 20.3 %fusion.22 = f32[16,256,256]{2,0,1:T(8,128)S(1)} fusion(f32[176,256,256]{1,0,2:T(8,128)} %copy.11, s32[176]{0:T(256)S(1)} %bitcast.65), kind=kOutput, calls=%fused_computation.30 | convolution fusion | flops 2214595328 | bytes 50332352 | tf_op jit(solution)/shard_map/bt,tik->bik/dot_general | solution.py:56
  250.3 4.4 copy.10
  255.0 61.9 %reduce-scatter.2.cloned.1.call-done = f32[1024,256]{1,0:T(8,128)} async-done(((f32[4096,256]{1,0:T(8,128)}), f32[1024,256]{1,0:T(8,128)}) %reduce-scatter.2.cloned.1.call-update) | async-done | bytes 1048592 | tf_op jit(solution)/shard_map/reduce_scatter | solution.py:58
  316.8 4.2 fusion.29
  321.0 107.0 %all-gather.3.cloned.1.call-done = f32[32768,256]{1,0:T(8,128)} async-done(((f32[256,256]{1,0:T(8,128)}), f32[32768,256]{1,0:T(8,128)}) %all-gather.3.cloned.1.call-update) | async-done | bytes 33554448 | tf_op jit(solution)/shard_map/all_gather | solution.py:60
  428.0 12.0 reduce_sum.9
  440.1 505.4 %while.33 = (s32[]{:T(128)}, f32[256,256]{1,0:T(8,128)S(1)}, f32[256,256]{1,0:T(8,128)S(1)}, s32[]{:T(128)}, s32[]{:T(128)}) while((s32[]{:T(128)}, f32[256,256]{1,0:T(8,128)S(1)}, f32[256,256]{1,0:T(8,128)S(1)}, s32[]{:T(128)}, s32[]{:T(128)}) %tuple.80), condition=%wide.region_3.4_spmd.clone.clone, body=%wide.region_2.3_spmd.clone.clone.sunk | while | flops 1902083 | bytes 1063021 | solution.py:22
  945.5 0.7 broadcast_multiply_fusion
  946.2 427.2 %while.32 = (s32[]{:T(128)}, f32[256,256]{1,0:T(8,128)S(1)}, f32[256,256]{1,0:T(8,128)S(1)}, s32[]{:T(128)}, s32[]{:T(128)}, /*index=5*/s32[]{:T(128)}, s32[]{:T(128)}) while((s32[]{:T(128)}, f32[256,256]{1,0:T(8,128)S(1)}, f32[256,256]{1,0:T(8,128)S(1)}, s32[]{:T(128)}, s32[]{:T(128)}, /*index=5*/s32[]{:T(128)}, s32[]{:T(128)}) %tuple.83), condition=%wide.region_5.6_spmd.clone, body=%wide.region_4.5_spmd.clone.sunk | while | flops 984328 | bytes 792242 | solution.py:37
  948.1 0.7 dynamic_slice.50
  949.7 0.7 dynamic_slice.50
  951.4 0.7 dynamic_slice.50
  953.1 0.7 dynamic_slice.50
  954.7 0.7 dynamic_slice.50
  956.4 0.7 dynamic_slice.50
  958.1 0.7 dynamic_slice.50
  1373.4 2.0 convolution_multiply_fusion
  (3600 shorter events, 723.5 us)
Async XLA Ops:
  7.2 1.2 copy-start
  7.2 16.4 %copy-start.5 = (s32[176,1]{0,1:T(1,128)S(1)}, s32[176,1]{0,1:T(1,128)}, u32[]{:S(2)}) copy-start(s32[176,1]{0,1:T(1,128)} %param.12) | copy-start | bytes 2116
  7.2 16.4 %copy-start.4 = (s32[176,1]{0,1:T(1,128)S(1)}, s32[176,1]{0,1:T(1,128)}, u32[]{:S(2)}) copy-start(s32[176,1]{0,1:T(1,128)} %param.13) | copy-start | bytes 2116
  13.9 118.2 %all-to-all-start = ((bf16[32,2,256,256]{3,2,1,0:T(8,128)(2,1)}), bf16[32,2,256,256]{3,2,1,0:T(8,128)(2,1)}, u32[]{:S(2)}, u32[]{:S(2)}) async-start(bf16[32,2,256,256]{3,2,1,0:T(8,128)(2,1)} %bitcast.58), calls=%async_computation | async-start | bytes 16777216 | tf_op jit(solution)/shard_map/all_to_all | solution.py:49
  23.6 293.2 %reduce-scatter.2.cloned.1.call-start = ((), (), s32[]{:S(2)}) async-start(), calls=%async_computation.2 | async-start | bytes 5242880 | tf_op jit(solution)/shard_map/reduce_scatter | solution.py:58
  183.5 46.5 %copy-start.3 = (s32[176,1]{0,1:T(1,128)S(1)}, s32[176,1]{0,1:T(1,128)}, u32[]{:S(2)}) copy-start(s32[176,1]{0,1:T(1,128)} %param.11) | copy-start | bytes 2116
  254.7 173.3 %all-gather.3.cloned.1.call-start = ((), (), s32[]{:S(2)}) async-start(), calls=%async_computation.3 | async-start | bytes 33816576 | tf_op jit(solution)/shard_map/all_gather | solution.py:60
  316.8 1056.6 %copy-start.2 = (f32[1024,256]{1,0:T(8,128)S(1)}, f32[1024,256]{1,0:T(8,128)}, u32[]{:S(2)}) copy-start(f32[1024,256]{1,0:T(8,128)} %reduce-scatter.2.cloned.1.call-done) | copy-start | bytes 3145732
  428.0 947.4 %copy-start.1 = (bf16[8,1,256,256]{3,2,1,0:T(8,128)(2,1)S(1)}, bf16[8,1,256,256]{3,2,1,0:T(8,128)(2,1)}, u32[]{:S(2)}) copy-start(bf16[8,1,256,256]{3,2,1,0:T(8,128)(2,1)} %param.15) | copy-start | bytes 3145732
Sparse Core Ops, SparseCore 0:
  254.9 61.9 reduce-scatter.1
  321.1 106.8 all-gather.2

commit v2 on v0

--- a/solution.py
+++ b/solution.py
@@ -57,7 +57,7 @@
     partial_value = partial_value.reshape(-1, rank_width)
     local_y = lax.psum_scatter(partial_value, "col", scatter_dimension=0, tiled=True)
     gram = jnp.dot(local_y.T, local_y, precision=lax.Precision.HIGHEST)
-    summed = lax.psum(gram, ("row", "col"))
+    summed = lax.psum(lax.psum(gram, "row"), "col")
     upper = upper_factor(summed)
     cells_all = local_y.shape[0] * lax.axis_size("row") * lax.axis_size("col")
     scale = jnp.sqrt(jnp.float32(cells_all))

time: 1600 us -> 1580 us (0.988)
  loops' own time: 202 us -> 182 us
    another operation x1, loops' own time: 189 us -> 170 us  [upper_factor(): lax.fori_loop(0, width, row_fill, jnp.zeros((width, width), jnp.float32))]
    psum x1 -> x2, waiting for transfers between devices: 143 us -> 143 us  [local(): summed = lax.psum(lax.psum(gram, 'row'), 'col')]
  transfers between devices with their start and end apart: 3 -> 4, of which waited for: 3 -> 4; matrix products, arithmetic and copies ran while one was open for 0% -> 0% of each run, Pallas kernels for 0% -> 0%
where the time goes in v2:
time: 1580 us; the launch traced here: 1560 us
  local copies, waits for them, and re-layouts  577 us (37%)
  waiting for transfers between devices  313 us (20%)
  matrix products  233 us (15%)
  other arithmetic  227 us (14%)
  loops' own time  182 us (12%)
    dynamic_slice x256, local copies, waits for them, and re-layouts, row_fill(): target = lax.dynamic_index_in_dim(gram, j, 0, keepdims=False)  190 us
    another operation x1, loops' own time, upper_factor(): lax.fori_loop(0, width, row_fill, jnp.zeros((width, width), jnp.float32))  170 us
    dynamic_slice x256, local copies, waits for them, and re-layouts, row_step(): pivot = lax.dynamic_index_in_dim(row_now, i, 0, keepdims=False)  164 us
    div x256, other arithmetic, row_step(): (unit - jnp.dot(row_now, inverse, precision=lax.Precision.HIGHEST)) / pivot  163 us
    dynamic_slice x256, local copies, waits for them, and re-layouts, row_fill(): pivot = jnp.sqrt(lax.dynamic_index_in_dim(residue, j, 0, keepdims=False))  151 us
    psum x2, waiting for transfers between devices, local(): summed = lax.psum(lax.psum(gram, 'row'), 'col')  143 us
    all_to_all x1, waiting for transfers between devices, local(): lax.all_to_all(outgoing, 'row', split_axis=0, concat_axis=0, tiled=True)  108 us
    reduce_scatter x1, waiting for transfers between devices, local(): lax.psum_scatter(partial_value, 'col', scatter_dimension=0, tiled=True)  61.9 us
  transfers between devices with their start and end apart: 4, of which 4 were waited for; matrix products, arithmetic and copies ran while one was open for 0% of the time, Pallas kernels for 0%

profile of v2, /device:TPU:1, one launch (start us, length us, event | category | flops | bytes accessed | tf_op | source)
XLA Modules:
  0.0 1556.8 jit_solution(825358364358055254)
XLA Ops:
  7.2 0.8 compare_select_fusion.2
  8.4 5.5 gather_fusion
  13.9 9.6 all-to-all-start
  23.7 108.4 %all-to-all-done = bf16[32,2,256,256]{3,2,1,0:T(8,128)(2,1)} async-done(((bf16[32,2,256,256]{3,2,1,0:T(8,128)(2,1)}), bf16[32,2,256,256]{3,2,1,0:T(8,128)(2,1)}, u32[]{:S(2)}, u32[]{:S(2)}) %all-to-all-start) | async-done | bytes 8388640 | tf_op jit(solution)/shard_map/all_to_all | solution.py:49
  132.1 13.8 gather_fusion.1
  145.9 37.6 %fusion.24 = f32[176,256,256]{2,1,0:T(8,128)} fusion(bf16[176,256,256]{2,1,0:T(8,128)(2,1)} %gather_fusion.1, bf16[176,1,256,256]{3,2,1,0:T(8,128)(2,1)} %param.10), kind=kOutput, calls=%fused_computation.32 | convolution fusion | flops 5905580032 | bytes 92274688 | tf_op jit(solution)/shard_map/tij,tjk->tik/dot_general | solution.py:52
  183.5 46.6 %copy.11 = f32[176,256,256]{1,0,2:T(8,128)} copy(f32[176,256,256]{2,1,0:T(8,128)} %fusion.24) | data formatting | bytes 92274688 | tf_op jit(solution)/shard_map/tij,tjk->tik/dot_general | solution.py:52
  230.1 20.4 %fusion.22 = f32[16,256,256]{2,0,1:T(8,128)S(1)} fusion(f32[176,256,256]{1,0,2:T(8,128)} %copy.11, s32[176]{0:T(256)S(1)} %bitcast.63), kind=kOutput, calls=%fused_computation.30 | convolution fusion | flops 2214595328 | bytes 50332352 | tf_op jit(solution)/shard_map/bt,tik->bik/dot_general | solution.py:56
  250.5 4.4 copy.10
  255.1 61.9 %reduce-scatter.2.cloned.1.call-done = f32[1024,256]{1,0:T(8,128)} async-done(((f32[4096,256]{1,0:T(8,128)}), f32[1024,256]{1,0:T(8,128)}) %reduce-scatter.2.cloned.1.call-update) | async-done | bytes 1048592 | tf_op jit(solution)/shard_map/reduce_scatter | solution.py:58
  317.0 4.1 fusion.29
  321.1 101.4 %all-reduce.3.cloned.1.call-done = f32[256,256]{1,0:T(8,128)} async-done(((f32[256,256]{1,0:T(8,128)}), f32[256,256]{1,0:T(8,128)}) %all-reduce.3.cloned.1.call-update) | async-done | bytes 262160 | tf_op jit(solution)/shard_map/psum | solution.py:60
  422.5 41.2 %all-reduce.5.cloned.1.call-done = f32[256,256]{1,0:T(8,128)} async-done(((f32[256,256]{1,0:T(8,128)}), f32[256,256]{1,0:T(8,128)}) %all-reduce.5.cloned.1.call-update) | async-done | bytes 262160 | tf_op jit(solution)/shard_map/psum | solution.py:60
  463.8 662.2 %while.33 = (s32[]{:T(128)}, f32[256,256]{1,0:T(8,128)S(1)}, f32[256,256]{1,0:T(8,128)}, s32[]{:T(128)}, s32[]{:T(128)}) while((s32[]{:T(128)}, f32[256,256]{1,0:T(8,128)S(1)}, f32[256,256]{1,0:T(8,128)}, s32[]{:T(128)}, s32[]{:T(128)}) %tuple.80), condition=%wide.region_4.5_spmd.clone.clone, body=%wide.region_3.4_spmd.clone.clone.sunk | while | flops 1902083 | bytes 1063021 | solution.py:22
  464.2 0.7 constant_dynamic-slice_fusion.2
  477.2 0.7 constant_dynamic-slice_fusion.2
  479.8 0.7 constant_dynamic-slice_fusion.2
  482.4 0.7 constant_dynamic-slice_fusion.2
  484.9 0.7 constant_dynamic-slice_fusion.2
  487.5 0.7 constant_dynamic-slice_fusion.2
  490.1 0.7 constant_dynamic-slice_fusion.2
  503.0 0.7 constant_dynamic-slice_fusion.2
  1126.7 420.4 %while.32 = (s32[]{:T(128)}, f32[256,256]{1,0:T(8,128)S(1)}, f32[256,256]{1,0:T(8,128)S(1)}, s32[]{:T(128)}, s32[]{:T(128)}, /*index=5*/s32[]{:T(128)}, s32[]{:T(128)}) while((s32[]{:T(128)}, f32[256,256]{1,0:T(8,128)S(1)}, f32[256,256]{1,0:T(8,128)S(1)}, s32[]{:T(128)}, s32[]{:T(128)}, /*index=5*/s32[]{:T(128)}, s32[]{:T(128)}) %tuple.83), condition=%wide.region_6.7_spmd.clone, body=%wide.region_5.6_spmd.clone.sunk | while | flops 984328 | bytes 792242 | solution.py:37
  1547.1 3.2 convolution_multiply_fusion
  (3600 shorter events, 895.9 us)
Async XLA Ops:
  7.2 1.2 copy-start
  7.2 16.4 %copy-start.4 = (s32[176,1]{0,1:T(1,128)S(1)}, s32[176,1]{0,1:T(1,128)}, u32[]{:S(2)}) copy-start(s32[176,1]{0,1:T(1,128)} %param.12) | copy-start | bytes 2116
  7.2 16.4 %copy-start.3 = (s32[176,1]{0,1:T(1,128)S(1)}, s32[176,1]{0,1:T(1,128)}, u32[]{:S(2)}) copy-start(s32[176,1]{0,1:T(1,128)} %param.13) | copy-start | bytes 2116
  13.9 118.2 %all-to-all-start = ((bf16[32,2,256,256]{3,2,1,0:T(8,128)(2,1)}), bf16[32,2,256,256]{3,2,1,0:T(8,128)(2,1)}, u32[]{:S(2)}, u32[]{:S(2)}) async-start(bf16[32,2,256,256]{3,2,1,0:T(8,128)(2,1)} %bitcast.57), calls=%async_computation | async-start | bytes 16777216 | tf_op jit(solution)/shard_map/all_to_all | solution.py:49
  23.6 293.4 %reduce-scatter.2.cloned.1.call-start = ((), (), s32[]{:S(2)}) async-start(), calls=%async_computation.2 | async-start | bytes 5242880 | tf_op jit(solution)/shard_map/reduce_scatter | solution.py:58
  183.5 46.6 %copy-start.2 = (s32[176,1]{0,1:T(1,128)S(1)}, s32[176,1]{0,1:T(1,128)}, u32[]{:S(2)}) copy-start(s32[176,1]{0,1:T(1,128)} %param.11) | copy-start | bytes 2116
  230.1 1320.2 %copy-start.1 = (bf16[8,1,256,256]{3,2,1,0:T(8,128)(2,1)S(1)}, bf16[8,1,256,256]{3,2,1,0:T(8,128)(2,1)}, u32[]{:S(2)}) copy-start(bf16[8,1,256,256]{3,2,1,0:T(8,128)(2,1)} %param.15) | copy-start | bytes 3145732
  254.9 167.6 %all-reduce.3.cloned.1.call-start = ((), (), s32[]{:S(2)}) async-start(), calls=%async_computation.3 | async-start | bytes 524288 | tf_op jit(solution)/shard_map/psum | solution.py:60
  321.1 142.7 %all-reduce.5.cloned.1.call-start = ((), (), s32[]{:S(2)}) async-start(), calls=%async_computation.4 | async-start | bytes 524288 | tf_op jit(solution)/shard_map/psum | solution.py:60
Sparse Core Ops, SparseCore 0:
  255.0 61.9 reduce-scatter.1
  321.2 101.2 all-reduce.2
  424.8 38.9 all-reduce.4
